TPU v7x, 256 devices: a whole 4x4x8 slice. The times are simulated.
256 devices in a mesh: walk: 8 (over x, core), pb: 32 (over z, y).
Axes of the slice: x: 4, y: 4, z: 8, core: 2. Of those that a mesh axis runs over, the one named last changes fastest.
Arguments:
- greens: bfloat16 [128, 64, 3072], P('walk', 'pb'), may hold values from -6 to 6
- cholesky: bfloat16 [128, 300, 3072], P('pb'), may hold values from -0.011962891 to 0.011962891
- slot_source: int32 [128], replicated, may hold values from 0 to 63, as said below
- block_transfer_index: int32 [128], P('pb'), may hold values from 0 to 15
- slot_multiplicity: int32 [128], P('pb'), may hold values from 0 to 3, as said below
- fields: float32 [128, 16, 300], P('walk'), may hold values from -6 to 6
- weight: float32 [128], P('walk'), may hold values from 0.2 to 5
Outputs:
- force_bias: float32 [128, 2, 4800], P('walk', None, 'pb')
- local_energy: float32 [128], P('walk')
- new_weight: float32 [128], P('walk')
- mixed_energy: float32 [], replicated
Inputs may be any that keep to these rules, and one draw needn't show every extreme that they name: `slot_source`: the Green's block of k-point k lies on index k // 2 of pb; with P = 32, slot j of pb index d (slot d * 4 + j) reads a block that lies on index (d + o_j) mod P of pb, where o_0 = 0, o_1 = P - 1, o_2 = 1, o_3 = P // 2. `slot_multiplicity`: 0 marks an empty slot; on each index of pb the live slots come first, and on some index all 4 slots are live.
All inputs are finite; a program needn't handle non-finite values.
Results may differ from a plain program's by a relative error of at most 0.0003.
Values may be sent and summed in bfloat16 or wider, within the bound.
No kernel may reach another device: no remote copies, remote signals or barrier semaphores. Data moves between devices by JAX's collectives and lax.ppermute only.
A program may use at most 320 MiB of HBM per device.

v0:
```python
import jax
import jax.numpy as jnp
from jax import lax
from jax.sharding import PartitionSpec as P

ORBITAL_COUNT = 96
OCCUPIED_COUNT = 16
TRANSFER_COUNT = 16


sqrt_step = 0.05


def slot_terms(chol_flat, green_flat):
    vectors = chol_flat.shape[0]
    walkers = green_flat.shape[0]
    doubled = 2 * ORBITAL_COUNT
    chol_block = chol_flat.reshape(vectors, OCCUPIED_COUNT, doubled)
    green_rows = green_flat.reshape(walkers, OCCUPIED_COUNT, doubled)
    real_part = green_rows[..., :ORBITAL_COUNT]
    imag_part = green_rows[..., ORBITAL_COUNT:]
    stacked = jnp.stack(
        [jnp.concatenate([real_part, -imag_part], -1), jnp.concatenate([imag_part, real_part], -1)],
        0,
    )
    left_matrix = chol_block.reshape(vectors * OCCUPIED_COUNT, doubled)
    right_matrix = stacked.reshape(2 * walkers * OCCUPIED_COUNT, doubled)
    product = lax.dot_general(
        left_matrix, right_matrix, (((1,), (1,)), ((), ())), preferred_element_type=jnp.float32
    )
    product = product.reshape(vectors, OCCUPIED_COUNT, 2, walkers, OCCUPIED_COUNT)
    identity = jnp.eye(OCCUPIED_COUNT, dtype=jnp.float32)
    diagonal = jnp.einsum("nicwj,ij->wcn", product, identity)
    crossed = jnp.einsum("nicwj,njcwi->cw", product, product)
    return (diagonal, crossed[0] - crossed[1])


def per_walker(bias_part, field_part):
    shift_real = sqrt_step * bias_part[:, 0]
    shift_imag = sqrt_step * bias_part[:, 1]
    coulomb = 0.5 * jnp.sum(
        bias_part[:, 0] * bias_part[:, 0] - bias_part[:, 1] * bias_part[:, 1], axis=1
    )
    real_arg = jnp.sum(
        field_part * shift_real - 0.5 * (shift_real * shift_real - shift_imag * shift_imag), axis=1
    )
    imag_arg = jnp.sum(field_part * shift_imag - shift_real * shift_imag, axis=1)
    return (coulomb, real_arg, imag_arg)


def local(greens, cholesky, slot_source, block_transfer_index, slot_multiplicity, fields, weight):
    group_list = lax.axis_size("pb")
    own_index = lax.axis_index("pb")
    slots_here = cholesky.shape[0]
    vectors = cholesky.shape[1]
    walkers = greens.shape[0]
    source_table = slot_source.reshape(group_list, slots_here)
    own_sources = lax.dynamic_index_in_dim(source_table, own_index, 0, keepdims=False)
    everything = lax.all_gather(greens, "pb", axis=1, tiled=True)
    bias = jnp.zeros((walkers, 2, TRANSFER_COUNT, vectors), jnp.float32)
    exchange_sum = jnp.zeros((walkers,), jnp.float32)

    def live_terms(operands):
        return slot_terms(operands[0], operands[1])

    def empty_terms(operands):
        return (jnp.zeros((walkers, 2, vectors), jnp.float32), jnp.zeros((walkers,), jnp.float32))

    for slot_index in range(slots_here):
        multiple_count = slot_multiplicity[slot_index]
        diagonal, crossed = lax.cond(
            multiple_count > 0,
            live_terms,
            empty_terms,
            (
                cholesky[slot_index],
                lax.dynamic_index_in_dim(everything, own_sources[slot_index], 1, keepdims=False),
            ),
        )
        scaled = multiple_count.astype(jnp.float32)
        factor = scaled * (jnp.arange(TRANSFER_COUNT) == block_transfer_index[slot_index]).astype(
            jnp.float32
        )
        bias = bias + factor[None, None, :, None] * diagonal[:, :, None, :]
        exchange_sum = exchange_sum + scaled * crossed
    flat_bias = bias.reshape(walkers, 2, TRANSFER_COUNT * vectors)
    flat_fields = fields.reshape(walkers, TRANSFER_COUNT * vectors)
    share_width = TRANSFER_COUNT * vectors // group_list
    total_bias, exchange_total = lax.psum((flat_bias, exchange_sum), "pb")
    coulomb, real_arg, imag_arg = per_walker(total_bias, flat_fields)
    bias_share = lax.dynamic_slice_in_dim(total_bias, own_index * share_width, share_width, 2)
    energy = coulomb - 0.5 * exchange_total
    new_weight = weight * jnp.exp(real_arg) * jnp.maximum(jnp.cos(imag_arg), 0.0)
    weighted_energy, weight_total = lax.psum((jnp.sum(weight * energy), jnp.sum(weight)), "walk")
    return (bias_share, energy, new_weight, weighted_energy / weight_total)


def solution(mesh):
    placed = (
        P("walk", "pb", None),
        P("pb", None, None),
        P(),
        P("pb"),
        P("pb"),
        P("walk", None, None),
        P("walk"),
    )
    return jax.shard_map(
        local,
        mesh=mesh,
        in_specs=placed,
        out_specs=(P("walk", None, "pb"), P("walk"), P("walk"), P()),
        check_vma=False,
    )
```

profile of v0, /device:TPU:1, one launch (start us, length us, event | category | flops | bytes accessed | tf_op | source)
XLA Modules:
  0.0 1177.3 jit_solution(733208971984589102)
XLA Ops:
  7.2 1.6 copy.28
  8.9 1.4 fusion.6
  15.5 0.8 reshape.156
  16.3 1.5 fusion.5
  19.8 0.7 mul.216
  22.6 0.7 mul.192
  23.3 79.5 %all-gather.2.cloned.1.call-done = bf16[16,64,3072]{2,0,1:T(8,128)(2,1)} async-done(((bf16[16,2,3072]{2,0,1:T(8,128)(2,1)}), bf16[16,64,3072]{2,0,1:T(8,128)(2,1)}) %all-gather.2.cloned.1.call-update) | async-done | bytes 6291472 | tf_op jit(solution)/shard_map/all_gather | solution.py:59
  102.9 0.8 copy.36
  104.3 0.8 copy.34
  105.1 226.5 %conditional.4 = (f32[16,2,300]{0,1,2:T(2,128)S(1)}, f32[16]{0:T(128)S(1)}) conditional(s32[]{:T(128)} %bitcast.42, () %tuple.64, (s32[1,4]{1,0:T(1,128)S(1)}, bf16[16,64,3072]{2,0,1:T(8,128)(2,1)}, bf16[4,300,3072]{2,0,1:T(4,128)(2,1)}) %tuple.70), branch_computations={%region_0.1_spmd, %region_1.2_spmd} | conditional | flops 954055808 | bytes 104218488 | solution.py:71
  110.9 0.9 constant_dynamic-slice_fusion
  112.3 5.3 copy.29
  117.7 1.4 slice.174
  119.1 4.1 reshape_squeeze.16
  123.2 5.2 convolution_bitcast_fusion
  128.4 44.4 %reshape.145 = f32[300,16,2,16,16]{4,3,2,1,0:T(8,128)} reshape(f32[4800,512]{1,0:T(8,128)} %convolution_bitcast_fusion) | data formatting | bytes 19660800 | tf_op jit(solution)/shard_map/cond/branch_1_fun/reshape | solution.py:31
  172.8 24.6 %multiply_reduce_fusion.1 = f32[300,2,16]{2,1,0:T(2,128)S(1)} fusion(f32[300,16,2,16,16]{4,3,2,1,0:T(8,128)} %reshape.145, f32[16,16]{1,0:T(8,128)S(1)} %fusion), kind=kLoop, calls=%fused_computation.1 | loop fusion | flops 4905600 | bytes 9869824 | tf_op jit(solution)/shard_map/cond/branch_1_fun/nicwj,ij->wcn/dot_general | solution.py:33
  197.4 86.4 %copy.48 = f32[2,16,16,16,300]{2,1,0,3,4:T(8,128)} copy(f32[2,16,16,16,300]{3,1,0,2,4:T(8,128)} %bitcast.1) | data formatting | bytes 19660800 | tf_op jit(solution)/shard_map/cond
  283.8 47.7 %multiply_reduce_fusion = f32[2,16]{1,0:T(2,128)S(1)} fusion(f32[2,16,16,16,300]{2,1,0,3,4:T(8,128)} %copy.48, f32[300,16,2,16,16]{4,3,2,1,0:T(8,128)} %reshape.145), kind=kLoop, calls=%fused_computation | loop fusion | flops 4915168 | bytes 19660928 | tf_op jit(solution)/shard_map/cond/branch_1_fun/nicwj,njcwi->cw/dot_general | solution.py:34
  331.8 6.5 conditional.5
  338.6 0.9 mul.203
  339.5 0.9 mul.195
  340.5 0.9 mul.211
  341.4 0.9 mul.219
  342.4 1.4 multiply_add_fusion
  343.8 714.8 %psum.29 = f32[16]{0:T(128)S(1)} all-reduce(f32[16]{0:T(128)S(1)} %multiply_add_fusion.1), channel_id=1, replica_groups=mesh['walk'=8,'pb'=32] {'pb'}, use_global_device_ids=true, to_apply=%region_10.11 | all-reduce | flops 16 | bytes 128 | tf_op jit(solution)/shard_map/psum | solution.py:89
  1058.6 83.3 %all-reduce.3.cloned.1.call-done = f32[16,2,4800]{2,1,0:T(2,128)} async-done(((f32[16,2,4800]{2,1,0:T(2,128)}), f32[16,2,4800]{2,1,0:T(2,128)}) %all-reduce.3.cloned.1.call-update) | async-done | bytes 614416 | tf_op jit(solution)/shard_map/psum | solution.py:89
  1141.9 3.6 multiply_reduce_fusion.8
  1146.1 1.3 subtract_reduce_fusion.1
  1147.4 1.2 fusion.4
  1148.5 17.7 %all-reduce = (f32[]{:T(128)}, f32[]{:T(128)}) all-reduce(f32[]{:T(128)} %get-tuple-element.250, f32[]{:T(128)} %get-tuple-element.249), channel_id=1, replica_groups=mesh['walk'=8,'pb'=32] {'walk'}, use_global_device_ids=true, to_apply=%region_14.15 | all-reduce | flops 2 | bytes 16 | tf_op jit(solution)/shard_map/psum | solution.py:94
  1167.6 1.5 constant_dynamic-slice_fusion.4
  (60 shorter events, 6.8 us)
Async XLA Ops:
  7.2 95.6 %all-gather.2.cloned.1.call-start = ((), (), s32[]{:S(2)}) async-start(), calls=%async_computation | async-start | bytes 6488064 | tf_op jit(solution)/shard_map/all_gather | solution.py:59
  8.9 1133.0 %all-reduce.3.cloned.1.call-start = ((), (), s32[]{:S(2)}) async-start(), calls=%async_computation.1 | async-start | bytes 1245184 | tf_op jit(solution)/shard_map/psum | solution.py:89
  102.9 0.8 copy-start.7
  104.3 0.8 copy-start.9
  331.7 8.7 copy-start.1
  331.8 9.6 copy-start
  331.8 10.6 copy-start.2
  331.8 10.6 copy-start.3
  331.8 10.6 copy-start.4
  331.8 10.6 copy-start.5
  338.3 5.4 copy-start.8
  338.4 5.4 copy-start.10
  338.4 809.0 %copy-start.6 = (f32[16]{0:T(128)S(1)}, f32[16]{0:T(128)}, u32[]{:S(2)}) copy-start(f32[16]{0:T(128)} %param.21) | copy-start | bytes 196
Sparse Core Ops, SparseCore 0:
  10.6 92.1 all-gather.1
  343.9 797.9 all-reduce.2
where the time goes:
time: 1200 us; the launch traced here: 1180 us
  blocking collectives  732 us (61%)
  waiting for transfers between devices  163 us (14%)
  local copies, waits for them, and re-layouts  159 us (13%)
  other arithmetic  82.6 us (7%)
  between operations  22.3 us (2%)
  loops' own time  12.9 us (1%)
    psum x1, blocking collectives, local(): total_bias, exchange_total = lax.psum((flat_bias, exchange_sum), 'pb')  715 us
    cond x1, local copies, waits for them, and re-layouts  86.4 us
    psum x1, waiting for transfers between devices, local(): total_bias, exchange_total = lax.psum((flat_bias, exchange_sum), 'pb')  83.3 us
    all_gather x1, waiting for transfers between devices, local(): everything = lax.all_gather(greens, 'pb', axis=1, tiled=True)  79.5 us
    dot_general x1, other arithmetic, slot_terms(): crossed = jnp.einsum('nicwj,njcwi->cw', product, product)  47.7 us
    reshape x1, local copies, waits for them, and re-layouts, slot_terms(): product.reshape(vectors, OCCUPIED_COUNT, 2, walkers, OCCUPIED_COUNT)  44.4 us
    dot_general x1, other arithmetic, slot_terms(): diagonal = jnp.einsum('nicwj,ij->wcn', product, identity)  24.6 us
  transfers between devices with their start and end apart: 2, of which 2 were waited for; matrix products, arithmetic and copies ran while one was open for 1% of the time, Pallas kernels for 0%

commit v1 on v0

v1 whole, which is shorter than its diff:
```python
import functools

import jax
import jax.numpy as jnp
from jax import lax
from jax.experimental import pallas as pl
from jax.experimental.pallas import tpu as pltpu
from jax.sharding import PartitionSpec as P

Q_ORB = 96
OCC = 16
CHOL = 300
TRANSFERS = 16
SLOTS = 4
DOUBLED = 2 * Q_ORB
FLAT = OCC * DOUBLED
WALKERS = 16
HALF = CHOL // 2
ROWS = 304
ROW_COUNT = 10
STEP = 0.05
F32 = jnp.float32
BF16 = jnp.bfloat16
NT = (((1,), (1,)), ((), ()))
VMEM = pl.BlockSpec(memory_space=pltpu.VMEM)


def pick_kernel(source_ref, green_ref, *out_refs):
    parts = lax.axis_size("pb")
    own = lax.axis_index("pb")
    lane = lax.broadcasted_iota(jnp.int32, (1, parts * SLOTS), 1)
    source = lax.rem(source_ref[...], 2).astype(F32)
    first = green_ref[:, 0, :].astype(F32)
    second = green_ref[:, 1, :].astype(F32)
    for j, out_ref in enumerate(out_refs):
        reader = lax.rem(own + parts - offset_of(j, parts), parts)
        kpoint = jnp.sum(jnp.where(lane == reader * SLOTS + j, source, 0.0), keepdims=True)
        out_ref[...] = jnp.where(kpoint < 0.5, first, second).astype(BF16)


def offset_of(j, parts):
    return (0, parts - 1, 1, parts // 2)[j]


def pick_call(source, greens):
    return pl.pallas_call(
        pick_kernel,
        out_shape=(jax.ShapeDtypeStruct((WALKERS, FLAT), BF16),) * SLOTS,
        in_specs=[VMEM, VMEM],
        out_specs=(VMEM,) * SLOTS,
        compiler_params=pltpu.CompilerParams(vmem_limit_bytes=4 * 2**20),
        name="pick",
    )(source, greens)


def build_right(green, right_ref):
    window = lax.broadcasted_iota(jnp.int32, (WALKERS, 256), 1)
    for c, plain in enumerate(signed_swapped(green)):
        moved = pltpu.roll(plain, 64, 1)
        for j in range(OCC):
            if j % 2 == 0:
                low = plain[:, j * DOUBLED : j * DOUBLED + 256]
                high = moved[:, j * DOUBLED : j * DOUBLED + 256]
            else:
                high = plain[:, j * DOUBLED - 64 : j * DOUBLED + 192]
                at = j * DOUBLED + 64
                if at + 256 <= FLAT:
                    low = moved[:, at : at + 256]
                else:
                    low = jnp.concatenate([moved[:, at:], moved[:, :128]], 1)
            low = jnp.where(window < DOUBLED, low, 0.0).astype(BF16)
            high = jnp.where(window >= 64, high, 0.0).astype(BF16)
            b, r = divmod(j, 4)
            for p in range(4):
                start = b * 128 + (r ^ p) * 32 + c * 16
                right_ref[p, start : start + 16, :] = low if p % 2 == 0 else high


def signed_swapped(green):
    wide = green.astype(F32)
    lane = lax.broadcasted_iota(jnp.int32, (WALKERS, FLAT), 1)
    first = lax.rem(lane, DOUBLED) < Q_ORB
    swapped = jnp.where(
        first, pltpu.roll(wide, FLAT - Q_ORB, 1), pltpu.roll(wide, Q_ORB, 1)
    )
    signed = jnp.where(first, wide, -wide)
    return signed, swapped


def diag_kernel(slots, chained, facts_ref, *refs):
    greens, rest = refs[: len(slots)], refs[len(slots) :]
    if chained:
        before_ref, chol_ref, out_ref, diag_ref = rest
        out_ref[...] = before_ref[...]
    else:
        chol_ref, out_ref, diag_ref = rest
    diag_ref[CHOL - 4 :, :] = jnp.zeros((512 - CHOL + 4, 128), F32)
    lane = lax.broadcasted_iota(jnp.int32, (16, 128), 1)
    more = HALF - 128
    spill = {}
    for at, slot in enumerate(slots):
        right = jnp.concatenate(signed_swapped(greens[at][...]), 0).astype(BF16)
        diag_ref[0:CHOL, 0:32] = lax.dot_general(
            chol_ref[slot], right, NT, preferred_element_type=F32
        )
        mult = facts_ref[0:1, slot : slot + 1]
        transfer = facts_ref[0:1, SLOTS + slot : SLOTS + slot + 1]
        for h in range(2):
            turned = jnp.transpose(diag_ref[pl.ds(h * HALF, 256), :])
            for c in range(2):
                value = mult * turned[c * 16 : c * 16 + 16, :]
                k = slot * 2 + c
                out_ref[pl.ds(h * 16 * ROW_COUNT + k, 16, stride=ROW_COUNT), :] = value[:, :128]
                tail = jnp.where(
                    lane < more, value[:, 128:], jnp.where(lane == more, transfer, 0.0)
                )
                if k % 4:
                    tail = pltpu.roll(tail, 32 * (k % 4), 1)
                key = (h, k // 4)
                spill[key] = spill[key] + tail if key in spill else tail
    for (h, block), tail in spill.items():
        rows = pl.ds(h * 16 * ROW_COUNT + 8 + block, 16, stride=ROW_COUNT)
        if chained:
            tail = tail + before_ref[rows, :]
        out_ref[rows, :] = tail


def diag_call(slots, facts, greens, before, chol):
    chained = before is not None
    return pl.pallas_call(
        functools.partial(diag_kernel, slots, chained),
        out_shape=jax.ShapeDtypeStruct((32 * ROW_COUNT, 128), F32),
        in_specs=[VMEM] * (2 + len(slots) + chained),
        out_specs=VMEM,
        scratch_shapes=[pltpu.VMEM((512, 128), F32)],
        compiler_params=pltpu.CompilerParams(vmem_limit_bytes=8 * 2**20),
        cost_estimate=pl.CostEstimate(
            flops=len(slots) * 2 * CHOL * FLAT * 256,
            bytes_accessed=len(slots) * CHOL * FLAT * 2,
            transcendentals=0,
        ),
        name="diag",
    )(facts, *greens, *((before,) if chained else ()), chol)


def products(at, chol_ref, right_ref, prod_ref):
    def one(p, a):
        i = 4 * a + p
        start = i * DOUBLED - (64 if p % 2 else 0)
        prod_ref[4 * p + a, 0:CHOL, :] = lax.dot_general(
            chol_ref[at, :, start : start + 256], right_ref[p], NT, preferred_element_type=F32
        )

    return [functools.partial(one, p, a) for p in range(4) for a in range(4)]


def crossed(prod_ref, rows, lower, even, totals):
    once, twice = totals
    for a in range(4):
        for b in range(a, 4):
            x = [prod_ref[4 * p + a, rows, b * 128 : b * 128 + 128] for p in range(4)]
            if a == b:
                y = x
            else:
                y = [prod_ref[4 * r + b, rows, a * 128 : a * 128 + 128] for r in range(4)]
            y02 = jnp.where(lower, y[0], y[2])
            y20 = jnp.where(lower, y[2], y[0])
            y13 = jnp.where(lower, y[1], y[3])
            y31 = jnp.where(lower, y[3], y[1])
            z = (
                jnp.where(even, y02, y13),
                jnp.where(even, y13, y02),
                jnp.where(even, y20, y31),
                jnp.where(even, y31, y20),
            )
            part = (x[0] * z[0] + x[1] * z[1]) + (x[2] * z[2] + x[3] * z[3])
            if a == b:
                once = once + part
            else:
                twice = twice + part
    return once, twice


def exchange_kernel(slots, chained, facts_ref, *refs):
    greens, rest = refs[: len(slots)], refs[len(slots) :]
    if chained:
        before_ref, far_ref, out_ref, *scratch = rest
        total = before_ref[...]
    else:
        far_ref, out_ref, *scratch = rest
        total = jnp.zeros((8, 128), F32)
    chol_ref, sems, *scratch = scratch
    right_refs, prod_refs = scratch[:2], scratch[2:]
    copies = [
        pltpu.make_async_copy(far_ref.at[slot], chol_ref.at[at], sems.at[at])
        for at, slot in enumerate(slots)
    ]
    for copy in copies:
        copy.start()
    for copy in copies:
        copy.wait()
    for prod_ref in prod_refs:
        prod_ref[:, ROWS - 8 :, :] = jnp.zeros((16, 8, 512), F32)
    group = lax.broadcasted_iota(jnp.int32, (8, 128), 1) // 32
    lower = group < 2
    even = lax.rem(group, 2) == 0
    zero = jnp.zeros((8, 128), F32)
    chunks = ROWS // 8
    build_right(greens[0][...], right_refs[0])
    for at in range(len(slots) + 1):
        dots = []
        if at < len(slots):
            dots = products(at, chol_ref, right_refs[at % 2], prod_refs[at % 2])
        if at + 1 < len(slots):
            build_right(greens[at + 1][...], right_refs[(at + 1) % 2])
        sums = (zero, zero)
        if not dots:

            def step(k, sums):
                rows = pl.ds(pl.multiple_of(k * 8, 8), 8)
                return crossed(prod_refs[(at + 1) % 2], rows, lower, even, sums)

            sums = lax.fori_loop(0, chunks, step, sums)
        done = 0
        for n, dot in enumerate(dots):
            dot()
            if at:
                upto = (n + 1) * chunks // len(dots)
                for k in range(done, upto):
                    sums = crossed(
                        prod_refs[(at + 1) % 2], slice(8 * k, 8 * k + 8), lower, even, sums
                    )
                done = upto
        if at:
            mult = facts_ref[0:1, slots[at - 1] : slots[at - 1] + 1]
            total = total + mult * (sums[0] + 2.0 * sums[1])
    out_ref[...] = total


def exchange_call(slots, facts, greens, before, chol):
    chained = before is not None
    return pl.pallas_call(
        functools.partial(exchange_kernel, slots, chained),
        out_shape=jax.ShapeDtypeStruct((8, 128), F32),
        in_specs=[VMEM] * (1 + len(slots) + chained)
        + [pl.BlockSpec(memory_space=pl.ANY)],
        out_specs=VMEM,
        scratch_shapes=[
            pltpu.VMEM((len(slots), CHOL, FLAT), BF16),
            pltpu.SemaphoreType.DMA((len(slots),)),
        ]
        + [pltpu.VMEM((4, 512, 256), BF16)] * 2
        + [pltpu.VMEM((16, ROWS, 512), F32)] * 2,
        compiler_params=pltpu.CompilerParams(vmem_limit_bytes=48 * 2**20),
        cost_estimate=pl.CostEstimate(
            flops=len(slots) * 4 * CHOL * 16 * 256 * 512,
            bytes_accessed=len(slots) * CHOL * FLAT * 2,
            transcendentals=0,
        ),
        name="exchange",
    )(facts, *greens, *((before,) if chained else ()), chol)


def share_kernel(got_ref, field_ref, exch_ref, out_ref):
    lane = lax.broadcasted_iota(jnp.int32, (TRANSFERS, 256), 1)
    which = lax.broadcasted_iota(jnp.int32, (128, TRANSFERS), 1).astype(F32)
    more = HALF - 128
    tails = [got_ref[pl.ds(8 + block, 32, stride=ROW_COUNT), :] for block in range(2)]
    rows = []
    for k in range(2 * SLOTS):
        tail = tails[k // 4]
        if k % 4:
            tail = pltpu.roll(tail, 128 - 32 * (k % 4), 1)
        head = got_ref[pl.ds(k, 32, stride=ROW_COUNT), :]
        rows.append(jnp.concatenate([head, tail], 1))
    even = jnp.concatenate(rows[0::2], 0)
    odd = jnp.concatenate(rows[1::2], 0)
    pick = jnp.where(even[:, HALF : HALF + 1] == which, 1.0, 0.0)
    bias = []
    for part in (even, odd):
        total = lax.dot_general(
            pick,
            part,
            (((0,), (0,)), ((), ())),
            precision=lax.Precision.HIGHEST,
            preferred_element_type=F32,
        )
        bias.append(jnp.where(lane < HALF, total, 0.0))
    real, imag = bias
    field = field_ref[...]
    shift_real = STEP * real
    shift_imag = STEP * imag
    terms = (
        0.5 * (real * real - imag * imag),
        field * shift_real - 0.5 * (shift_real * shift_real - shift_imag * shift_imag),
        field * shift_imag - shift_real * shift_imag,
    )
    head = lax.broadcasted_iota(jnp.int32, (1, 128), 1)
    row = jnp.zeros((1, 128), F32)
    for k, term in enumerate(terms):
        row = row + jnp.where(head == 64 + k, jnp.sum(term, keepdims=True), 0.0)
    exch = jnp.sum(exch_ref[...], axis=0, keepdims=True)
    mixed = real[:, 128:] + pltpu.roll(imag[:, 128:], 32, 1) + row
    for ho in range(2):
        for k, line in enumerate((real[:, :128], imag[:, :128], mixed)):
            out_ref[pl.ds(4 * ho + k, 16, stride=8), :] = line
    out_ref[pl.ds(3, 32, stride=4), :] = jnp.broadcast_to(exch, (32, 128))


def share_call(got, field, exch):
    return pl.pallas_call(
        share_kernel,
        out_shape=jax.ShapeDtypeStruct((128, 128), F32),
        compiler_params=pltpu.CompilerParams(vmem_limit_bytes=8 * 2**20),
        name="share",
    )(got, field, exch)


def final_kernel(got_ref, weight_ref, energy_ref, real_ref, imag_ref, pair_ref):
    scalars = got_ref[pl.ds(2, 32, stride=4), :]
    exch = jnp.sum(got_ref[pl.ds(3, 32, stride=4), :], axis=0, keepdims=True)
    exch = jnp.broadcast_to(exch, (8, 128))
    exch = exch + pltpu.roll(exch, 64, 1)
    exch = exch + pltpu.roll(exch, 32, 1)
    exch = exch - pltpu.roll(exch, 128 - WALKERS, 1)
    both = scalars[0:WALKERS] + scalars[WALKERS : 2 * WALKERS]
    lane = lax.broadcasted_iota(jnp.int32, (WALKERS, 128), 1)
    own = lane == lax.broadcasted_iota(jnp.int32, (WALKERS, 128), 0)
    coulomb, real_arg, imag_arg = (
        jnp.sum(jnp.where(own, both[:, k : k + 1], 0.0), axis=0, keepdims=True)
        for k in range(64, 67)
    )
    head = lane[0:1] < WALKERS
    energy = jnp.where(head, coulomb - 0.5 * exch[0:1], 0.0)
    weight = jnp.where(head, weight_ref[...], 0.0)
    top = jnp.sum(weight * energy, keepdims=True)
    bottom = jnp.sum(weight, keepdims=True)
    energy_ref[...] = energy[:, :WALKERS]
    real_ref[...] = real_arg[:, :WALKERS]
    imag_ref[...] = imag_arg[:, :WALKERS]
    pair_ref[...] = jnp.where(lax.broadcasted_iota(jnp.int32, (8, 128), 1) == 0, top, bottom)


def final_call(got, weight):
    return pl.pallas_call(
        final_kernel,
        out_shape=(jax.ShapeDtypeStruct((1, WALKERS), F32),) * 3
        + (jax.ShapeDtypeStruct((8, 128), F32),),
        compiler_params=pltpu.CompilerParams(vmem_limit_bytes=4 * 2**20),
        name="final",
    )(got, weight)


def mixed_kernel(pair_ref, out_ref):
    total = jnp.sum(pair_ref[...], axis=0, keepdims=True)
    out_ref[...] = total[:, 0:1] / total[:, 1:2]


def mixed_call(pair):
    return pl.pallas_call(
        mixed_kernel,
        out_shape=jax.ShapeDtypeStruct((1, 1), F32),
        compiler_params=pltpu.CompilerParams(vmem_limit_bytes=4 * 2**20),
        name="mixed",
    )(pair)


def local(greens, cholesky, slot_source, block_transfer_index, slot_multiplicity, fields, weight):
    parts = lax.axis_size("pb")
    own = lax.axis_index("pb")
    blocks = list(pick_call(slot_source.reshape(1, -1), greens))
    for j in (1, 3, 2):
        offset = offset_of(j, parts)
        pairs = [(d, (d + parts - offset) % parts) for d in range(parts)]
        blocks[j] = lax.ppermute(blocks[j], "pb", pairs)
    half, walker = own // WALKERS, lax.rem(own, WALKERS)
    field = lax.dynamic_index_in_dim(fields, walker, 0, keepdims=False)
    field = lax.dynamic_slice_in_dim(field, half * HALF, HALF, 1)
    field = jnp.pad(field, ((0, 0), (0, 256 - HALF)))

    facts = jnp.concatenate([slot_multiplicity, block_transfer_index]).astype(F32)
    facts = jnp.pad(facts, (0, 128 - 2 * SLOTS)).reshape(1, 128)
    sent = diag_call((0, 1, 2), facts, blocks[:3], None, cholesky)
    sent = diag_call((3,), facts, blocks[3:], sent, cholesky)
    got = lax.all_to_all(sent.reshape(parts, ROW_COUNT, 1, 128), "pb", 0, 0, tiled=True)
    exch = exchange_call((0, 1, 2, 3), facts, blocks, None, cholesky)
    shared = share_call(got.reshape(parts * ROW_COUNT, 128), field, exch)
    final = lax.all_to_all(shared.reshape(parts, 4, 1, 128), "pb", 0, 0, tiled=True)

    wide_weight = jnp.pad(weight, (0, 128 - WALKERS)).reshape(1, 128)
    energy, real_arg, imag_arg, pair = final_call(final.reshape(128, 128), wide_weight)
    pair = lax.all_to_all(pair.reshape(8, 1, 128), "walk", 0, 0, tiled=True)
    mixed = mixed_call(pair.reshape(8, 128)).reshape(())
    mine = lax.dynamic_slice_in_dim(
        final.reshape(parts, 4, 128), lax.rem(own, 2) * WALKERS, WALKERS, 0
    )
    more = HALF - 128
    bias = jnp.stack(
        [jnp.concatenate([mine[:, c], mine[:, 2, 32 * c : 32 * c + more]], 1) for c in range(2)], 1
    )
    energy, real_arg, imag_arg = (x.reshape(WALKERS) for x in (energy, real_arg, imag_arg))
    new_weight = weight * jnp.exp(real_arg) * jnp.maximum(jnp.cos(imag_arg), 0.0)
    return (bias, energy, new_weight, mixed)


def solution(mesh):
    placed = (
        P("walk", "pb", None),
        P("pb", None, None),
        P(),
        P("pb"),
        P("pb"),
        P("walk", None, None),
        P("walk"),
    )
    return jax.shard_map(
        local,
        mesh=mesh,
        in_specs=placed,
        out_specs=(P("walk", None, "pb"), P("walk"), P("walk"), P()),
        check_vma=False,
    )
```

time: 1200 us -> 75.1 us (0.06); the launches traced: 1180 us -> 74.8 us
  blocking collectives: 732 us -> 0 us
  local copies, waits for them, and re-layouts: 159 us -> 7.82 us
  waiting for transfers between devices: 163 us -> 12.2 us
  other arithmetic: 82.6 us -> 0.65 us
  starting transfers between devices: 0.08 us -> 33.9 us
  between operations: 22.3 us -> 0.81 us
  Pallas kernels: 0 us -> 19.5 us
  loops' own time: 12.9 us -> 0 us
    psum x2 -> x0, blocking collectives: 732 us -> none  [the longest x1 715 us: local(): total_bias, exchange_total = lax.psum((flat_bias, exchange_sum), 'pb')]
    cond x5 -> x0, local copies, waits for them, and re-layouts: 88.3 us -> none
    psum x1 -> x0, waiting for transfers between devices: 83.3 us -> none  [local(): total_bias, exchange_total = lax.psum((flat_bias, exchange_sum), 'pb')]
    all_gather x1 -> x0, waiting for transfers between devices: 79.5 us -> none  [local(): everything = lax.all_gather(greens, 'pb', axis=1, tiled=True)]
    dot_general x2 -> x0, other arithmetic: 72.4 us -> none  [the longest x1 47.7 us: slot_terms(): crossed = jnp.einsum('nicwj,njcwi->cw', product, product)]
    reshape x3 -> x2, local copies, waits for them, and re-layouts: 45.3 us -> 0.01 us  [the longest x1 0.01 us: local(): wide_weight = jnp.pad(weight, (0, 128 - WALKERS)).reshape(1, 128)]
    all_to_all x0 -> x3, starting transfers between devices: none -> 21.3 us  [the longest x1 9.04 us: local(): lax.all_to_all(shared.reshape(parts, 4, 1, 128), 'pb', 0, 0, tiled=True)]
    pallas_call x0 -> x7, Pallas kernels: none -> 19.5 us  [the longest x1 11.7 us: exchange_call(): pl.pallas_call(functools.partial(exchange_kernel, slots, chained), out_sh...]
  transfers between devices with their start and end apart: 2 -> 6, of which waited for: 2 -> 2; matrix products, arithmetic and copies ran while one was open for 1% -> 9% of each run, Pallas kernels for 0% -> 18%
where the time goes in v1:
time: 75.1 us; the launch traced here: 74.8 us
  starting transfers between devices  33.9 us (45%)
  Pallas kernels  19.5 us (26%)
  waiting for transfers between devices  12.2 us (16%)
  local copies, waits for them, and re-layouts  7.82 us (10%)
  between operations  0.81 us (1%)
    ppermute x3, starting transfers between devices, local(): blocks[j] = lax.ppermute(blocks[j], 'pb', pairs)  12.6 us
    pallas_call x1, Pallas kernels, exchange_call(): pl.pallas_call(functools.partial(exchange_kernel, slots, chained), out_sh...  11.7 us
    all_to_all x1, starting transfers between devices, local(): lax.all_to_all(shared.reshape(parts, 4, 1, 128), 'pb', 0, 0, tiled=True)  9.04 us
    all_to_all x1, waiting for transfers between devices, local(): lax.all_to_all(shared.reshape(parts, 4, 1, 128), 'pb', 0, 0, tiled=True)  8.8 us
    unnamed x16, local copies, waits for them, and re-layouts  7.64 us
    all_to_all x1, starting transfers between devices, local(): pair = lax.all_to_all(pair.reshape(8, 1, 128), 'walk', 0, 0, tiled=True)  7.44 us
    all_to_all x1, starting transfers between devices, local(): lax.all_to_all(sent.reshape(parts, ROW_COUNT, 1, 128), 'pb', 0, 0, tiled=...  4.78 us
    pallas_call x2, Pallas kernels, diag_call(): pl.pallas_call(functools.partial(diag_kernel, slots, chained), out_shape=...  3.61 us
  transfers between devices with their start and end apart: 6, of which 2 were waited for; matrix products, arithmetic and copies ran while one was open for 9% of the time, Pallas kernels for 18%

profile of v1, /device:TPU:1, one launch (start us, length us, event | category | flops | bytes accessed | tf_op | source)
XLA Modules:
  0.0 74.8 jit_solution(9959454318169312744)
XLA Ops:
  0.6 0.0 copy-start
  0.7 1.0 %copy-done.2 = bf16[16,2,3072]{2,1,0:T(2,128)(2,1)S(1)} copy-done((bf16[16,2,3072]{2,1,0:T(2,128)(2,1)S(1)}, bf16[16,2,3072]{2,1,0:T(2,128)(2,1)}, u32[]{:S(2)}) %copy-start.2) | copy-done | bytes 196632
  1.6 0.7 copy-done.3
  2.3 1.5 %pick.1 = (bf16[16,3072]{1,0:T(8,128)(2,1)S(1)}, bf16[16,3072]{1,0:T(8,128)(2,1)S(1)}, bf16[16,3072]{1,0:T(8,128)(2,1)S(1)}, bf16[16,3072]{1,0:T(8,128)(2,1)S(1)}) custom-call(s32[1,128]{1,0:T(1,128)S(1)} %bitcast.43, bf16[16,2,3072]{2,1,0:T(2,128)(2,1)S(1)} %copy-done.2), custom_call_target="tpu_custom_call" | custom-call | tf_op jit(solution)/shard_map/pick/pallas_call | solution.py:46
  3.8 0.0 copy-start.5
  3.8 0.0 copy-start.6
  3.8 7.8 %collective-permute-start = (bf16[16,3072]{1,0:T(8,128)(2,1)S(1)}, bf16[16,3072]{1,0:T(8,128)(2,1)S(1)}, u32[]{:S(2)}, u32[]{:S(2)}) collective-permute-start(bf16[16,3072]{1,0:T(8,128)(2,1)S(1)} %get-tuple-element.12), channel_id=1, source_target_pairs={{0,16},{1,17},{2,18},{3,19},{4,20},{5,21},{6,22},{7,23},{8,24},{9,... | collective-permute-start | bytes 294920 | tf_op jit(solution)/shard_map/ppermute | solution.py:375
  11.6 1.3 %collective-permute-start.1 = (bf16[16,3072]{1,0:T(8,128)(2,1)S(1)}, bf16[16,3072]{1,0:T(8,128)(2,1)S(1)}, u32[]{:S(2)}, u32[]{:S(2)}) collective-permute-start(bf16[16,3072]{1,0:T(8,128)(2,1)S(1)} %get-tuple-element.14), channel_id=1, source_target_pairs={{0,1},{1,2},{2,3},{3,4},{4,5},{5,6},{6,7},{7,8},{8,9},{9,10},{10,1... | collective-permute-start | bytes 294920 | tf_op jit(solution)/shard_map/ppermute | solution.py:375
  12.9 3.5 %collective-permute-start.2 = (bf16[16,3072]{1,0:T(8,128)(2,1)S(1)}, bf16[16,3072]{1,0:T(8,128)(2,1)S(1)}, u32[]{:S(2)}, u32[]{:S(2)}) collective-permute-start(bf16[16,3072]{1,0:T(8,128)(2,1)S(1)} %get-tuple-element.15), channel_id=1, source_target_pairs={{0,31},{1,0},{2,1},{3,2},{4,3},{5,4},{6,5},{7,6},{8,7},{9,8},{10,9... | collective-permute-start | bytes 294920 | tf_op jit(solution)/shard_map/ppermute | solution.py:375
  16.4 5.3 %copy.21.refs_3_.refs_2_.refs_4_ = bf16[4,300,3072]{2,1,0:T(8,128)(2,1)S(1)} copy(bf16[4,300,3072]{2,0,1:T(4,128)(2,1)} %param.8) | data formatting | bytes 14745600 | tf_op args[1]
  21.8 0.0 copy-done.5
  21.8 0.1 add_convert_fusion
  21.9 0.1 dynamic-slice_bitcast_fusion
  22.0 0.0 collective-permute-done.1.refs_1_
  22.0 0.0 collective-permute-done.2.refs_2_
  22.0 2.0 %diag.2.refs_1_ = f32[320,128]{1,0:T(8,128)S(1)} custom-call(f32[1,128]{1,0:T(1,128)S(1)} %pad_bitcast_fusion.1.facts_ref, bf16[16,3072]{1,0:T(8,128)(2,1)S(1)} %get-tuple-element.13.refs_0_, bf16[16,3072]{1,0:T(8,128)(2,1)S(1)} %collective-permute-done.1.refs_1_, bf16[16,3072]{1,0:T(8,128)(2,1)S(1)} %collective-permute-done.2.refs_2_, ...), custom_call_target="tpu_custom_call" | custom-call | flops 1415577600 | bytes 5529600 | tf_op jit(solution)/shard_map/diag/pallas_call | solution.py:130
  24.0 0.0 collective-permute-done.refs_0_.refs_3_
  24.0 1.6 %diag.3 = f32[320,128]{1,0:T(8,128)} custom-call(f32[1,128]{1,0:T(1,128)S(1)} %pad_bitcast_fusion.1.facts_ref, bf16[16,3072]{1,0:T(8,128)(2,1)S(1)} %collective-permute-done.refs_0_.refs_3_, f32[320,128]{1,0:T(8,128)S(1)} %diag.2.refs_1_, bf16[4,300,3072]{2,1,0:T(8,128)(2,1)S(1)} %copy.21.refs_3_.refs_2_.refs_4_), custom_call_target="tpu_custom_call" | custom-call | flops 471859200 | bytes 1843200 | tf_op jit(solution)/shard_map/diag/pallas_call | solution.py:130
  25.6 4.8 %all-to-all-start = ((f32[32,10,1,128]{3,2,1,0:T(1,128)}), f32[32,10,1,128]{3,2,1,0:T(1,128)S(1)}, u32[]{:S(2)}, u32[]{:S(2)}) async-start(f32[32,10,1,128]{3,2,1,0:T(1,128)} %bitcast.2), calls=%async_computation | async-start | bytes 327680 | tf_op jit(solution)/shard_map/all_to_all | solution.py:385
  30.4 0.0 copy-start.4
  30.4 11.7 %exchange.1.exch_ref = f32[8,128]{1,0:T(8,128)S(1)} custom-call(f32[1,128]{1,0:T(1,128)S(1)} %pad_bitcast_fusion.1.facts_ref, bf16[16,3072]{1,0:T(8,128)(2,1)S(1)} %get-tuple-element.13.refs_0_, bf16[16,3072]{1,0:T(8,128)(2,1)S(1)} %collective-permute-done.1.refs_1_, bf16[16,3072]{1,0:T(8,128)(2,1)S(1)} %collective-permute-done.2.refs_2_, ...), custom_call_target="tpu_custom_call" | custom-call | flops 10066329600 | bytes 7372800 | tf_op jit(solution)/shard_map/exchange/pallas_call | solution.py:242
  42.2 0.0 all-to-all-done
  42.2 1.1 %share.1 = f32[128,128]{1,0:T(8,128)} custom-call(f32[320,128]{1,0:T(8,128)S(1)} %bitcast.40, f32[16,256]{1,0:T(8,128)S(1)} %pad.13.field_ref, f32[8,128]{1,0:T(8,128)S(1)} %exchange.1.exch_ref), custom_call_target="tpu_custom_call" | custom-call | tf_op jit(solution)/shard_map/share/pallas_call | solution.py:311
  43.3 9.0 %all-to-all-start.1 = ((f32[32,4,1,128]{3,1,2,0:T(4,128)}), f32[32,4,1,128]{3,1,2,0:T(4,128)S(1)}, u32[]{:S(2)}, u32[]{:S(2)}) async-start(f32[32,4,1,128]{3,1,2,0:T(4,128)} %bitcast.6), calls=%async_computation.1 | async-start | bytes 131072 | tf_op jit(solution)/shard_map/all_to_all | solution.py:388
  52.4 8.8 %all-to-all-done.1 = f32[32,4,1,128]{3,1,2,0:T(4,128)S(1)} async-done(((f32[32,4,1,128]{3,1,2,0:T(4,128)}), f32[32,4,1,128]{3,1,2,0:T(4,128)S(1)}, u32[]{:S(2)}, u32[]{:S(2)}) %all-to-all-start.1) | async-done | bytes 65568 | tf_op jit(solution)/shard_map/all_to_all | solution.py:388
  61.2 0.1 slice_bitcast_fusion.2
  61.3 0.9 %final.1 = (f32[1,16]{1,0:T(1,128)}, f32[1,16]{1,0:T(1,128)S(1)}, f32[1,16]{1,0:T(1,128)S(1)}, f32[8,128]{1,0:T(8,128)}) custom-call(f32[128,128]{1,0:T(8,128)S(1)} %bitcast.41, f32[1,128]{1,0:T(1,128)S(1)} %pad_bitcast_fusion.weight_ref), custom_call_target="tpu_custom_call" | custom-call | tf_op jit(solution)/shard_map/final/pallas_call | solution.py:345
  62.2 7.4 %all-to-all-start.2 = ((f32[8,1,128]{2,1,0:T(1,128)}), f32[8,1,128]{2,1,0:T(1,128)S(1)}, u32[]{:S(2)}, u32[]{:S(2)}) async-start(f32[8,1,128]{2,1,0:T(1,128)} %bitcast.20), calls=%async_computation.2 | async-start | bytes 8192 | tf_op jit(solution)/shard_map/all_to_all | solution.py:392
  69.7 0.6 bitcast_multiply_fusion
  70.2 0.6 copy.28
  70.9 3.4 %all-to-all-done.2 = f32[8,1,128]{2,1,0:T(1,128)S(1)} async-done(((f32[8,1,128]{2,1,0:T(1,128)}), f32[8,1,128]{2,1,0:T(1,128)S(1)}, u32[]{:S(2)}, u32[]{:S(2)}) %all-to-all-start.2) | async-done | bytes 4128 | tf_op jit(solution)/shard_map/all_to_all | solution.py:392
  74.2 0.6 mixed.1
  (15 shorter events, 0.1 us)
Async XLA Ops:
  0.6 21.2 %copy-start = (f32[16,16,300]{2,1,0:T(8,128)S(1)}, f32[16,16,300]{2,1,0:T(8,128)}, u32[]{:S(2)}) copy-start(f32[16,16,300]{2,1,0:T(8,128)} %param.12) | copy-start | bytes 921604
  0.6 1.0 %copy-start.2 = (bf16[16,2,3072]{2,1,0:T(2,128)(2,1)S(1)}, bf16[16,2,3072]{2,1,0:T(2,128)(2,1)}, u32[]{:S(2)}) copy-start(bf16[16,2,3072]{2,1,0:T(2,128)(2,1)} %green_ref.1) | copy-start | bytes 589828
  1.6 0.7 copy-start.3
  3.8 18.0 %copy-start.5 = (s32[4]{0:T(128)S(1)}, s32[4]{0:T(128)}, u32[]{:S(2)}) copy-start(s32[4]{0:T(128)} %param.10) | copy-start | bytes 52
  3.8 18.0 %copy-start.6 = (s32[4]{0:T(128)S(1)}, s32[4]{0:T(128)}, u32[]{:S(2)}) copy-start(s32[4]{0:T(128)} %param.11) | copy-start | bytes 52
  3.8 20.2 %collective-permute-start = (bf16[16,3072]{1,0:T(8,128)(2,1)S(1)}, bf16[16,3072]{1,0:T(8,128)(2,1)S(1)}, u32[]{:S(2)}, u32[]{:S(2)}) collective-permute-start(bf16[16,3072]{1,0:T(8,128)(2,1)S(1)} %get-tuple-element.12), channel_id=1, source_target_pairs={{0,16},{1,17},{2,18},{3,19},{4,20},{5,21},{6,22},{7,23},{8,24},{9,... | collective-permute-start | bytes 294920 | tf_op jit(solution)/shard_map/ppermute | solution.py:375
  11.6 10.3 %collective-permute-start.1 = (bf16[16,3072]{1,0:T(8,128)(2,1)S(1)}, bf16[16,3072]{1,0:T(8,128)(2,1)S(1)}, u32[]{:S(2)}, u32[]{:S(2)}) collective-permute-start(bf16[16,3072]{1,0:T(8,128)(2,1)S(1)} %get-tuple-element.14), channel_id=1, source_target_pairs={{0,1},{1,2},{2,3},{3,4},{4,5},{5,6},{6,7},{7,8},{8,9},{9,10},{10,1... | collective-permute-start | bytes 294920 | tf_op jit(solution)/shard_map/ppermute | solution.py:375
  12.9 9.1 %collective-permute-start.2 = (bf16[16,3072]{1,0:T(8,128)(2,1)S(1)}, bf16[16,3072]{1,0:T(8,128)(2,1)S(1)}, u32[]{:S(2)}, u32[]{:S(2)}) collective-permute-start(bf16[16,3072]{1,0:T(8,128)(2,1)S(1)} %get-tuple-element.15), channel_id=1, source_target_pairs={{0,31},{1,0},{2,1},{3,2},{4,3},{5,4},{6,5},{7,6},{8,7},{9,8},{10,9... | collective-permute-start | bytes 294920 | tf_op jit(solution)/shard_map/ppermute | solution.py:375
  21.8 3.8 %copy-start.1 = (bf16[4,300,3072]{2,1,0:T(8,128)(2,1)}, bf16[4,300,3072]{2,1,0:T(8,128)(2,1)S(1)}, u32[]{:S(2)}) copy-start(bf16[4,300,3072]{2,1,0:T(8,128)(2,1)S(1)} %copy.21.refs_3_.refs_2_.refs_4_) | copy-start | bytes 22118404
  25.6 16.6 %all-to-all-start = ((f32[32,10,1,128]{3,2,1,0:T(1,128)}), f32[32,10,1,128]{3,2,1,0:T(1,128)S(1)}, u32[]{:S(2)}, u32[]{:S(2)}) async-start(f32[32,10,1,128]{3,2,1,0:T(1,128)} %bitcast.2), calls=%async_computation | async-start | bytes 327680 | tf_op jit(solution)/shard_map/all_to_all | solution.py:385
  30.4 22.0 %copy-start.4 = (f32[16]{0:T(128)S(1)}, f32[16]{0:T(128)}, u32[]{:S(2)}) copy-start(f32[16]{0:T(128)} %param.13) | copy-start | bytes 196
  43.3 17.9 %all-to-all-start.1 = ((f32[32,4,1,128]{3,1,2,0:T(4,128)}), f32[32,4,1,128]{3,1,2,0:T(4,128)S(1)}, u32[]{:S(2)}, u32[]{:S(2)}) async-start(f32[32,4,1,128]{3,1,2,0:T(4,128)} %bitcast.6), calls=%async_computation.1 | async-start | bytes 131072 | tf_op jit(solution)/shard_map/all_to_all | solution.py:388
  62.2 12.0 %all-to-all-start.2 = ((f32[8,1,128]{2,1,0:T(1,128)}), f32[8,1,128]{2,1,0:T(1,128)S(1)}, u32[]{:S(2)}, u32[]{:S(2)}) async-start(f32[8,1,128]{2,1,0:T(1,128)} %bitcast.20), calls=%async_computation.2 | async-start | bytes 8192 | tf_op jit(solution)/shard_map/all_to_all | solution.py:392

commit v2 on v1

--- a/solution.py
+++ b/solution.py
@@ -120,7 +120,7 @@
                 spill[key] = spill[key] + tail if key in spill else tail
     for (h, block), tail in spill.items():
         rows = pl.ds(h * 16 * ROW_COUNT + 8 + block, 16, stride=ROW_COUNT)
-        if chained:
+        if chained and 2 * block < slots[0]:
             tail = tail + before_ref[rows, :]
         out_ref[rows, :] = tail
 
@@ -220,7 +220,7 @@
                 rows = pl.ds(pl.multiple_of(k * 8, 8), 8)
                 return crossed(prod_refs[(at + 1) % 2], rows, lower, even, sums)
 
-            sums = lax.fori_loop(0, chunks, step, sums)
+            sums = lax.fori_loop(0, chunks, step, sums, unroll=38)
         done = 0
         for n, dot in enumerate(dots):
             dot()
@@ -380,8 +380,8 @@
 
     facts = jnp.concatenate([slot_multiplicity, block_transfer_index]).astype(F32)
     facts = jnp.pad(facts, (0, 128 - 2 * SLOTS)).reshape(1, 128)
-    sent = diag_call((0, 1, 2), facts, blocks[:3], None, cholesky)
-    sent = diag_call((3,), facts, blocks[3:], sent, cholesky)
+    sent = diag_call((0,), facts, blocks[:1], None, cholesky)
+    sent = diag_call((1, 2, 3), facts, blocks[1:], sent, cholesky)
     got = lax.all_to_all(sent.reshape(parts, ROW_COUNT, 1, 128), "pb", 0, 0, tiled=True)
     exch = exchange_call((0, 1, 2, 3), facts, blocks, None, cholesky)
     shared = share_call(got.reshape(parts * ROW_COUNT, 128), field, exch)

time: 75.1 us -> 74.5 us (level)
    unnamed x16 -> x12, local copies, waits for them, and re-layouts: 7.64 us -> 7.63 us
  transfers between devices with their start and end apart: 6 -> 6, of which waited for: 2 -> 2; matrix products, arithmetic and copies ran while one was open for 9% -> 10% of each run, Pallas kernels for 18% -> 16%
where the time goes in v2:
time: 74.5 us; the launch traced here: 74.2 us
  starting transfers between devices  33.2 us (45%)
  Pallas kernels  18.9 us (25%)
  waiting for transfers between devices  12.2 us (16%)
  local copies, waits for them, and re-layouts  7.8 us (10%)
  other arithmetic  1.32 us (2%)
  between operations  0.79 us (1%)
    ppermute x3, starting transfers between devices, local(): blocks[j] = lax.ppermute(blocks[j], 'pb', pairs)  12.6 us
    pallas_call x1, Pallas kernels, exchange_call(): pl.pallas_call(functools.partial(exchange_kernel, slots, chained), out_sh...  11.2 us
    all_to_all x1, starting transfers between devices, local(): lax.all_to_all(shared.reshape(parts, 4, 1, 128), 'pb', 0, 0, tiled=True)  9.04 us
    all_to_all x1, waiting for transfers between devices, local(): lax.all_to_all(shared.reshape(parts, 4, 1, 128), 'pb', 0, 0, tiled=True)  8.79 us
    unnamed x12, local copies, waits for them, and re-layouts  7.63 us
    all_to_all x1, starting transfers between devices, local(): pair = lax.all_to_all(pair.reshape(8, 1, 128), 'walk', 0, 0, tiled=True)  7.51 us
    all_to_all x1, starting transfers between devices, local(): lax.all_to_all(sent.reshape(parts, ROW_COUNT, 1, 128), 'pb', 0, 0, tiled=...  4.04 us
    pallas_call x2, Pallas kernels, diag_call(): pl.pallas_call(functools.partial(diag_kernel, slots, chained), out_shape=...  3.55 us
  transfers between devices with their start and end apart: 6, of which 2 were waited for; matrix products, arithmetic and copies ran while one was open for 10% of the time, Pallas kernels for 16%

profile of v2, /device:TPU:1, one launch (start us, length us, event | category | flops | bytes accessed | tf_op | source)
XLA Modules:
  0.0 74.2 jit_solution(9649602590585490912)
XLA Ops:
  0.6 0.0 copy-start
  0.6 0.0 copy-start.2
  0.7 1.0 %copy-done.2 = bf16[16,2,3072]{2,1,0:T(2,128)(2,1)S(1)} copy-done((bf16[16,2,3072]{2,1,0:T(2,128)(2,1)S(1)}, bf16[16,2,3072]{2,1,0:T(2,128)(2,1)}, u32[]{:S(2)}) %copy-start.2) | copy-done | bytes 196632
  1.6 0.7 copy-done.3
  2.3 1.5 %pick.1 = (bf16[16,3072]{1,0:T(8,128)(2,1)S(1)}, bf16[16,3072]{1,0:T(8,128)(2,1)S(1)}, bf16[16,3072]{1,0:T(8,128)(2,1)S(1)}, bf16[16,3072]{1,0:T(8,128)(2,1)S(1)}) custom-call(s32[1,128]{1,0:T(1,128)S(1)} %bitcast.43, bf16[16,2,3072]{2,1,0:T(2,128)(2,1)S(1)} %copy-done.2), custom_call_target="tpu_custom_call" | custom-call | tf_op jit(solution)/shard_map/pick/pallas_call | solution.py:46
  3.8 2.2 %collective-permute-start = (bf16[16,3072]{1,0:T(8,128)(2,1)S(1)}, bf16[16,3072]{1,0:T(8,128)(2,1)S(1)}, u32[]{:S(2)}, u32[]{:S(2)}) collective-permute-start(bf16[16,3072]{1,0:T(8,128)(2,1)S(1)} %get-tuple-element.12), channel_id=1, source_target_pairs={{0,1},{1,2},{2,3},{3,4},{4,5},{5,6},{6,7},{7,8},{8,9},{9,10},{10,1... | collective-permute-start | bytes 294920 | tf_op jit(solution)/shard_map/ppermute | solution.py:375
  6.0 6.8 %collective-permute-start.1 = (bf16[16,3072]{1,0:T(8,128)(2,1)S(1)}, bf16[16,3072]{1,0:T(8,128)(2,1)S(1)}, u32[]{:S(2)}, u32[]{:S(2)}) collective-permute-start(bf16[16,3072]{1,0:T(8,128)(2,1)S(1)} %get-tuple-element.13), channel_id=1, source_target_pairs={{0,31},{1,0},{2,1},{3,2},{4,3},{5,4},{6,5},{7,6},{8,7},{9,8},{10,9... | collective-permute-start | bytes 294920 | tf_op jit(solution)/shard_map/ppermute | solution.py:375
  12.8 3.6 %collective-permute-start.2 = (bf16[16,3072]{1,0:T(8,128)(2,1)S(1)}, bf16[16,3072]{1,0:T(8,128)(2,1)S(1)}, u32[]{:S(2)}, u32[]{:S(2)}) collective-permute-start(bf16[16,3072]{1,0:T(8,128)(2,1)S(1)} %get-tuple-element.14), channel_id=1, source_target_pairs={{0,16},{1,17},{2,18},{3,19},{4,20},{5,21},{6,22},{7,23},{8,24},{9,... | collective-permute-start | bytes 294920 | tf_op jit(solution)/shard_map/ppermute | solution.py:375
  16.4 0.7 %add_convert_fusion = f32[8]{0:T(128)S(1)} fusion(s32[4]{0:T(128)} %param.10, s32[4]{0:T(128)} %param.11), kind=kLoop, calls=%fused_computation.9 | loop fusion | flops 16 | bytes 64 | tf_op jit(solution)/shard_map/convert_element_type | solution.py:381
  17.1 0.1 dynamic-slice_bitcast_fusion
  17.2 5.3 %copy.21.refs_1_.refs_4_ = bf16[4,300,3072]{2,1,0:T(8,128)(2,1)S(1)} copy(bf16[4,300,3072]{2,0,1:T(4,128)(2,1)} %param.8) | data formatting | bytes 14745600 | tf_op args[1]
  22.6 0.9 %diag.2.refs_3_ = f32[320,128]{1,0:T(8,128)S(1)} custom-call(f32[1,128]{1,0:T(1,128)S(1)} %pad_bitcast_fusion.1.facts_ref, bf16[16,3072]{1,0:T(8,128)(2,1)S(1)} %get-tuple-element.15.refs_0_, bf16[4,300,3072]{2,1,0:T(8,128)(2,1)S(1)} %copy.21.refs_1_.refs_4_), custom_call_target="tpu_custom_call" | custom-call | flops 471859200 | bytes 1843200 | tf_op jit(solution)/shard_map/diag/pallas_call | solution.py:130
  23.5 0.0 collective-permute-done.refs_0_.refs_1_
  23.5 0.0 collective-permute-done.1.refs_1_.refs_2_
  23.5 0.0 collective-permute-done.2.refs_2_.refs_3_
  23.5 2.7 %diag.3 = f32[320,128]{1,0:T(8,128)} custom-call(f32[1,128]{1,0:T(1,128)S(1)} %pad_bitcast_fusion.1.facts_ref, bf16[16,3072]{1,0:T(8,128)(2,1)S(1)} %collective-permute-done.refs_0_.refs_1_, bf16[16,3072]{1,0:T(8,128)(2,1)S(1)} %collective-permute-done.1.refs_1_.refs_2_, bf16[16,3072]{1,0:T(8,128)(2,1)S(1)} %collective-permute-done.2.refs_2_.refs_3_, ...), custom_call_target="tpu_custom_call" | custom-call | flops 1415577600 | bytes 5529600 | tf_op jit(solution)/shard_map/diag/pallas_call | solution.py:130
  26.2 0.0 copy-done.1
  26.2 4.0 %all-to-all-start = ((f32[32,10,1,128]{3,2,1,0:T(1,128)}), f32[32,10,1,128]{3,2,1,0:T(1,128)S(1)}, u32[]{:S(2)}, u32[]{:S(2)}) async-start(f32[32,10,1,128]{3,2,1,0:T(1,128)} %bitcast.2), calls=%async_computation | async-start | bytes 327680 | tf_op jit(solution)/shard_map/all_to_all | solution.py:385
  30.2 0.0 copy-start.4
  30.2 11.2 %exchange.1.exch_ref = f32[8,128]{1,0:T(8,128)S(1)} custom-call(f32[1,128]{1,0:T(1,128)S(1)} %pad_bitcast_fusion.1.facts_ref, bf16[16,3072]{1,0:T(8,128)(2,1)S(1)} %get-tuple-element.15.refs_0_, bf16[16,3072]{1,0:T(8,128)(2,1)S(1)} %collective-permute-done.refs_0_.refs_1_, bf16[16,3072]{1,0:T(8,128)(2,1)S(1)} %collective-permute-done.1.refs_1_.refs_2_, ...), custom_call_target="tpu_custom_call" | custom-call | flops 10066329600 | bytes 7372800 | tf_op jit(solution)/shard_map/exchange/pallas_call | solution.py:242
  41.4 0.0 all-to-all-done
  41.4 1.2 %share.1 = f32[128,128]{1,0:T(8,128)} custom-call(f32[320,128]{1,0:T(8,128)S(1)} %bitcast.40, f32[16,256]{1,0:T(8,128)S(1)} %pad.13.field_ref, f32[8,128]{1,0:T(8,128)S(1)} %exchange.1.exch_ref), custom_call_target="tpu_custom_call" | custom-call | tf_op jit(solution)/shard_map/share/pallas_call | solution.py:311
  42.6 9.0 %all-to-all-start.1 = ((f32[32,4,1,128]{3,1,2,0:T(4,128)}), f32[32,4,1,128]{3,1,2,0:T(4,128)S(1)}, u32[]{:S(2)}, u32[]{:S(2)}) async-start(f32[32,4,1,128]{3,1,2,0:T(4,128)} %bitcast.6), calls=%async_computation.1 | async-start | bytes 131072 | tf_op jit(solution)/shard_map/all_to_all | solution.py:388
  51.6 0.0 copy-done.4
  51.7 8.8 %all-to-all-done.1 = f32[32,4,1,128]{3,1,2,0:T(4,128)S(1)} async-done(((f32[32,4,1,128]{3,1,2,0:T(4,128)}), f32[32,4,1,128]{3,1,2,0:T(4,128)S(1)}, u32[]{:S(2)}, u32[]{:S(2)}) %all-to-all-start.1) | async-done | bytes 65568 | tf_op jit(solution)/shard_map/all_to_all | solution.py:388
  60.5 0.1 slice_bitcast_fusion.2
  60.5 0.9 %final.1 = (f32[1,16]{1,0:T(1,128)}, f32[1,16]{1,0:T(1,128)S(1)}, f32[1,16]{1,0:T(1,128)S(1)}, f32[8,128]{1,0:T(8,128)}) custom-call(f32[128,128]{1,0:T(8,128)S(1)} %bitcast.41, f32[1,128]{1,0:T(1,128)S(1)} %pad_bitcast_fusion.weight_ref), custom_call_target="tpu_custom_call" | custom-call | tf_op jit(solution)/shard_map/final/pallas_call | solution.py:345
  61.5 7.5 %all-to-all-start.2 = ((f32[8,1,128]{2,1,0:T(1,128)}), f32[8,1,128]{2,1,0:T(1,128)S(1)}, u32[]{:S(2)}, u32[]{:S(2)}) async-start(f32[8,1,128]{2,1,0:T(1,128)} %bitcast.20), calls=%async_computation.2 | async-start | bytes 8192 | tf_op jit(solution)/shard_map/all_to_all | solution.py:392
  69.0 0.6 bitcast_multiply_fusion
  69.6 0.6 copy.28
  70.2 3.4 %all-to-all-done.2 = f32[8,1,128]{2,1,0:T(1,128)S(1)} async-done(((f32[8,1,128]{2,1,0:T(1,128)}), f32[8,1,128]{2,1,0:T(1,128)S(1)}, u32[]{:S(2)}, u32[]{:S(2)}) %all-to-all-start.2) | async-done | bytes 4128 | tf_op jit(solution)/shard_map/all_to_all | solution.py:392
  73.6 0.6 mixed.1
  (11 shorter events, 0.0 us)
Async XLA Ops:
  0.6 16.5 %copy-start = (f32[16,16,300]{2,1,0:T(8,128)S(1)}, f32[16,16,300]{2,1,0:T(8,128)}, u32[]{:S(2)}) copy-start(f32[16,16,300]{2,1,0:T(8,128)} %param.12) | copy-start | bytes 921604
  0.6 1.0 %copy-start.2 = (bf16[16,2,3072]{2,1,0:T(2,128)(2,1)S(1)}, bf16[16,2,3072]{2,1,0:T(2,128)(2,1)}, u32[]{:S(2)}) copy-start(bf16[16,2,3072]{2,1,0:T(2,128)(2,1)} %green_ref.1) | copy-start | bytes 589828
  1.6 0.7 copy-start.3
  3.8 19.7 %collective-permute-start = (bf16[16,3072]{1,0:T(8,128)(2,1)S(1)}, bf16[16,3072]{1,0:T(8,128)(2,1)S(1)}, u32[]{:S(2)}, u32[]{:S(2)}) collective-permute-start(bf16[16,3072]{1,0:T(8,128)(2,1)S(1)} %get-tuple-element.12), channel_id=1, source_target_pairs={{0,1},{1,2},{2,3},{3,4},{4,5},{5,6},{6,7},{7,8},{8,9},{9,10},{10,1... | collective-permute-start | bytes 294920 | tf_op jit(solution)/shard_map/ppermute | solution.py:375
  6.0 17.5 %collective-permute-start.1 = (bf16[16,3072]{1,0:T(8,128)(2,1)S(1)}, bf16[16,3072]{1,0:T(8,128)(2,1)S(1)}, u32[]{:S(2)}, u32[]{:S(2)}) collective-permute-start(bf16[16,3072]{1,0:T(8,128)(2,1)S(1)} %get-tuple-element.13), channel_id=1, source_target_pairs={{0,31},{1,0},{2,1},{3,2},{4,3},{5,4},{6,5},{7,6},{8,7},{9,8},{10,9... | collective-permute-start | bytes 294920 | tf_op jit(solution)/shard_map/ppermute | solution.py:375
  12.8 10.7 %collective-permute-start.2 = (bf16[16,3072]{1,0:T(8,128)(2,1)S(1)}, bf16[16,3072]{1,0:T(8,128)(2,1)S(1)}, u32[]{:S(2)}, u32[]{:S(2)}) collective-permute-start(bf16[16,3072]{1,0:T(8,128)(2,1)S(1)} %get-tuple-element.14), channel_id=1, source_target_pairs={{0,16},{1,17},{2,18},{3,19},{4,20},{5,21},{6,22},{7,23},{8,24},{9,... | collective-permute-start | bytes 294920 | tf_op jit(solution)/shard_map/ppermute | solution.py:375
  22.6 3.6 %copy-start.1 = (bf16[4,300,3072]{2,1,0:T(8,128)(2,1)}, bf16[4,300,3072]{2,1,0:T(8,128)(2,1)S(1)}, u32[]{:S(2)}) copy-start(bf16[4,300,3072]{2,1,0:T(8,128)(2,1)S(1)} %copy.21.refs_1_.refs_4_) | copy-start | bytes 22118404
  26.2 15.2 %all-to-all-start = ((f32[32,10,1,128]{3,2,1,0:T(1,128)}), f32[32,10,1,128]{3,2,1,0:T(1,128)S(1)}, u32[]{:S(2)}, u32[]{:S(2)}) async-start(f32[32,10,1,128]{3,2,1,0:T(1,128)} %bitcast.2), calls=%async_computation | async-start | bytes 327680 | tf_op jit(solution)/shard_map/all_to_all | solution.py:385
  30.2 21.4 %copy-start.4 = (f32[16]{0:T(128)S(1)}, f32[16]{0:T(128)}, u32[]{:S(2)}) copy-start(f32[16]{0:T(128)} %param.13) | copy-start | bytes 196
  42.6 17.9 %all-to-all-start.1 = ((f32[32,4,1,128]{3,1,2,0:T(4,128)}), f32[32,4,1,128]{3,1,2,0:T(4,128)S(1)}, u32[]{:S(2)}, u32[]{:S(2)}) async-start(f32[32,4,1,128]{3,1,2,0:T(4,128)} %bitcast.6), calls=%async_computation.1 | async-start | bytes 131072 | tf_op jit(solution)/shard_map/all_to_all | solution.py:388
  61.5 12.1 %all-to-all-start.2 = ((f32[8,1,128]{2,1,0:T(1,128)}), f32[8,1,128]{2,1,0:T(1,128)S(1)}, u32[]{:S(2)}, u32[]{:S(2)}) async-start(f32[8,1,128]{2,1,0:T(1,128)} %bitcast.20), calls=%async_computation.2 | async-start | bytes 8192 | tf_op jit(solution)/shard_map/all_to_all | solution.py:392

commit v3 on v2

--- a/solution.py
+++ b/solution.py
@@ -18,6 +18,7 @@
 HALF = CHOL // 2
 ROWS = 304
 ROW_COUNT = 10
+LANE_CUTS = 2
 STEP = 0.05
 F32 = jnp.float32
 BF16 = jnp.bfloat16
@@ -191,9 +192,15 @@
         total = jnp.zeros((8, 128), F32)
     chol_ref, sems, *scratch = scratch
     right_refs, prod_refs = scratch[:2], scratch[2:]
+    width = FLAT // LANE_CUTS
     copies = [
-        pltpu.make_async_copy(far_ref.at[slot], chol_ref.at[at], sems.at[at])
+        pltpu.make_async_copy(
+            far_ref.at[slot, :, cut * width : (cut + 1) * width],
+            chol_ref.at[at, :, cut * width : (cut + 1) * width],
+            sems.at[at, cut],
+        )
         for at, slot in enumerate(slots)
+        for cut in range(LANE_CUTS)
     ]
     for copy in copies:
         copy.start()
@@ -247,7 +254,7 @@
         out_specs=VMEM,
         scratch_shapes=[
             pltpu.VMEM((len(slots), CHOL, FLAT), BF16),
-            pltpu.SemaphoreType.DMA((len(slots),)),
+            pltpu.SemaphoreType.DMA((len(slots), LANE_CUTS)),
         ]
         + [pltpu.VMEM((4, 512, 256), BF16)] * 2
         + [pltpu.VMEM((16, ROWS, 512), F32)] * 2,

time: 74.5 us -> 74.5 us (level)
  no operation moved by 1% of the time
where the time goes in v3:
time: 74.5 us; the launch traced here: 74.1 us
  starting transfers between devices  33.2 us (45%)
  Pallas kernels  18.9 us (25%)
  waiting for transfers between devices  12.2 us (16%)
  local copies, waits for them, and re-layouts  7.8 us (10%)
  other arithmetic  1.32 us (2%)
  between operations  0.79 us (1%)
    ppermute x3, starting transfers between devices, local(): blocks[j] = lax.ppermute(blocks[j], 'pb', pairs)  12.6 us
    pallas_call x1, Pallas kernels, exchange_call(): pl.pallas_call(functools.partial(exchange_kernel, slots, chained), out_sh...  11.1 us
    all_to_all x1, starting transfers between devices, local(): lax.all_to_all(shared.reshape(parts, 4, 1, 128), 'pb', 0, 0, tiled=True)  9.04 us
    all_to_all x1, waiting for transfers between devices, local(): lax.all_to_all(shared.reshape(parts, 4, 1, 128), 'pb', 0, 0, tiled=True)  8.79 us
    unnamed x12, local copies, waits for them, and re-layouts  7.63 us
    all_to_all x1, starting transfers between devices, local(): pair = lax.all_to_all(pair.reshape(8, 1, 128), 'walk', 0, 0, tiled=True)  7.52 us
    all_to_all x1, starting transfers between devices, local(): lax.all_to_all(sent.reshape(parts, ROW_COUNT, 1, 128), 'pb', 0, 0, tiled=...  4.04 us
    pallas_call x2, Pallas kernels, diag_call(): pl.pallas_call(functools.partial(diag_kernel, slots, chained), out_shape=...  3.55 us
  transfers between devices with their start and end apart: 6, of which 2 were waited for; matrix products, arithmetic and copies ran while one was open for 10% of the time, Pallas kernels for 16%

profile of v3, /device:TPU:1, one launch (start us, length us, event | category | flops | bytes accessed | tf_op | source)
XLA Modules:
  0.0 74.1 jit_solution(11672279169070413697)
XLA Ops:
  0.6 0.0 copy-start
  0.6 0.0 copy-start.2
  0.7 1.0 %copy-done.2 = bf16[16,2,3072]{2,1,0:T(2,128)(2,1)S(1)} copy-done((bf16[16,2,3072]{2,1,0:T(2,128)(2,1)S(1)}, bf16[16,2,3072]{2,1,0:T(2,128)(2,1)}, u32[]{:S(2)}) %copy-start.2) | copy-done | bytes 196632
  1.6 0.7 copy-done.3
  2.3 1.5 %pick.1 = (bf16[16,3072]{1,0:T(8,128)(2,1)S(1)}, bf16[16,3072]{1,0:T(8,128)(2,1)S(1)}, bf16[16,3072]{1,0:T(8,128)(2,1)S(1)}, bf16[16,3072]{1,0:T(8,128)(2,1)S(1)}) custom-call(s32[1,128]{1,0:T(1,128)S(1)} %bitcast.43, bf16[16,2,3072]{2,1,0:T(2,128)(2,1)S(1)} %copy-done.2), custom_call_target="tpu_custom_call" | custom-call | tf_op jit(solution)/shard_map/pick/pallas_call | solution.py:47
  3.8 2.2 %collective-permute-start = (bf16[16,3072]{1,0:T(8,128)(2,1)S(1)}, bf16[16,3072]{1,0:T(8,128)(2,1)S(1)}, u32[]{:S(2)}, u32[]{:S(2)}) collective-permute-start(bf16[16,3072]{1,0:T(8,128)(2,1)S(1)} %get-tuple-element.12), channel_id=1, source_target_pairs={{0,1},{1,2},{2,3},{3,4},{4,5},{5,6},{6,7},{7,8},{8,9},{9,10},{10,1... | collective-permute-start | bytes 294920 | tf_op jit(solution)/shard_map/ppermute | solution.py:382
  6.0 6.8 %collective-permute-start.1 = (bf16[16,3072]{1,0:T(8,128)(2,1)S(1)}, bf16[16,3072]{1,0:T(8,128)(2,1)S(1)}, u32[]{:S(2)}, u32[]{:S(2)}) collective-permute-start(bf16[16,3072]{1,0:T(8,128)(2,1)S(1)} %get-tuple-element.13), channel_id=1, source_target_pairs={{0,31},{1,0},{2,1},{3,2},{4,3},{5,4},{6,5},{7,6},{8,7},{9,8},{10,9... | collective-permute-start | bytes 294920 | tf_op jit(solution)/shard_map/ppermute | solution.py:382
  12.8 3.6 %collective-permute-start.2 = (bf16[16,3072]{1,0:T(8,128)(2,1)S(1)}, bf16[16,3072]{1,0:T(8,128)(2,1)S(1)}, u32[]{:S(2)}, u32[]{:S(2)}) collective-permute-start(bf16[16,3072]{1,0:T(8,128)(2,1)S(1)} %get-tuple-element.14), channel_id=1, source_target_pairs={{0,16},{1,17},{2,18},{3,19},{4,20},{5,21},{6,22},{7,23},{8,24},{9,... | collective-permute-start | bytes 294920 | tf_op jit(solution)/shard_map/ppermute | solution.py:382
  16.4 0.7 %add_convert_fusion = f32[8]{0:T(128)S(1)} fusion(s32[4]{0:T(128)} %param.10, s32[4]{0:T(128)} %param.11), kind=kLoop, calls=%fused_computation.9 | loop fusion | flops 16 | bytes 64 | tf_op jit(solution)/shard_map/convert_element_type | solution.py:388
  17.1 0.0 copy-done
  17.1 0.1 dynamic-slice_bitcast_fusion
  17.2 5.3 %copy.21.refs_1_.refs_4_ = bf16[4,300,3072]{2,1,0:T(8,128)(2,1)S(1)} copy(bf16[4,300,3072]{2,0,1:T(4,128)(2,1)} %param.8) | data formatting | bytes 14745600 | tf_op args[1]
  22.6 0.9 %diag.2.refs_3_ = f32[320,128]{1,0:T(8,128)S(1)} custom-call(f32[1,128]{1,0:T(1,128)S(1)} %pad_bitcast_fusion.1.facts_ref, bf16[16,3072]{1,0:T(8,128)(2,1)S(1)} %get-tuple-element.15.refs_0_, bf16[4,300,3072]{2,1,0:T(8,128)(2,1)S(1)} %copy.21.refs_1_.refs_4_), custom_call_target="tpu_custom_call" | custom-call | flops 471859200 | bytes 1843200 | tf_op jit(solution)/shard_map/diag/pallas_call | solution.py:131
  23.5 0.0 collective-permute-done.refs_0_.refs_1_
  23.5 0.0 collective-permute-done.1.refs_1_.refs_2_
  23.5 0.0 collective-permute-done.2.refs_2_.refs_3_
  23.5 2.7 %diag.3 = f32[320,128]{1,0:T(8,128)} custom-call(f32[1,128]{1,0:T(1,128)S(1)} %pad_bitcast_fusion.1.facts_ref, bf16[16,3072]{1,0:T(8,128)(2,1)S(1)} %collective-permute-done.refs_0_.refs_1_, bf16[16,3072]{1,0:T(8,128)(2,1)S(1)} %collective-permute-done.1.refs_1_.refs_2_, bf16[16,3072]{1,0:T(8,128)(2,1)S(1)} %collective-permute-done.2.refs_2_.refs_3_, ...), custom_call_target="tpu_custom_call" | custom-call | flops 1415577600 | bytes 5529600 | tf_op jit(solution)/shard_map/diag/pallas_call | solution.py:131
  26.2 0.0 copy-done.1
  26.2 4.0 %all-to-all-start = ((f32[32,10,1,128]{3,2,1,0:T(1,128)}), f32[32,10,1,128]{3,2,1,0:T(1,128)S(1)}, u32[]{:S(2)}, u32[]{:S(2)}) async-start(f32[32,10,1,128]{3,2,1,0:T(1,128)} %bitcast.2), calls=%async_computation | async-start | bytes 327680 | tf_op jit(solution)/shard_map/all_to_all | solution.py:392
  30.2 0.0 copy-start.4
  30.2 11.1 %exchange.1.exch_ref = f32[8,128]{1,0:T(8,128)S(1)} custom-call(f32[1,128]{1,0:T(1,128)S(1)} %pad_bitcast_fusion.1.facts_ref, bf16[16,3072]{1,0:T(8,128)(2,1)S(1)} %get-tuple-element.15.refs_0_, bf16[16,3072]{1,0:T(8,128)(2,1)S(1)} %collective-permute-done.refs_0_.refs_1_, bf16[16,3072]{1,0:T(8,128)(2,1)S(1)} %collective-permute-done.1.refs_1_.refs_2_, ...), custom_call_target="tpu_custom_call" | custom-call | flops 10066329600 | bytes 7372800 | tf_op jit(solution)/shard_map/exchange/pallas_call | solution.py:249
  41.4 0.0 all-to-all-done
  41.4 1.2 %share.1 = f32[128,128]{1,0:T(8,128)} custom-call(f32[320,128]{1,0:T(8,128)S(1)} %bitcast.40, f32[16,256]{1,0:T(8,128)S(1)} %pad.13.field_ref, f32[8,128]{1,0:T(8,128)S(1)} %exchange.1.exch_ref), custom_call_target="tpu_custom_call" | custom-call | tf_op jit(solution)/shard_map/share/pallas_call | solution.py:318
  42.6 9.0 %all-to-all-start.1 = ((f32[32,4,1,128]{3,1,2,0:T(4,128)}), f32[32,4,1,128]{3,1,2,0:T(4,128)S(1)}, u32[]{:S(2)}, u32[]{:S(2)}) async-start(f32[32,4,1,128]{3,1,2,0:T(4,128)} %bitcast.6), calls=%async_computation.1 | async-start | bytes 131072 | tf_op jit(solution)/shard_map/all_to_all | solution.py:395
  51.6 8.8 %all-to-all-done.1 = f32[32,4,1,128]{3,1,2,0:T(4,128)S(1)} async-done(((f32[32,4,1,128]{3,1,2,0:T(4,128)}), f32[32,4,1,128]{3,1,2,0:T(4,128)S(1)}, u32[]{:S(2)}, u32[]{:S(2)}) %all-to-all-start.1) | async-done | bytes 65568 | tf_op jit(solution)/shard_map/all_to_all | solution.py:395
  60.4 0.1 slice_bitcast_fusion.2
  60.5 0.9 %final.1 = (f32[1,16]{1,0:T(1,128)}, f32[1,16]{1,0:T(1,128)S(1)}, f32[1,16]{1,0:T(1,128)S(1)}, f32[8,128]{1,0:T(8,128)}) custom-call(f32[128,128]{1,0:T(8,128)S(1)} %bitcast.41, f32[1,128]{1,0:T(1,128)S(1)} %pad_bitcast_fusion.weight_ref), custom_call_target="tpu_custom_call" | custom-call | tf_op jit(solution)/shard_map/final/pallas_call | solution.py:352
  61.5 7.5 %all-to-all-start.2 = ((f32[8,1,128]{2,1,0:T(1,128)}), f32[8,1,128]{2,1,0:T(1,128)S(1)}, u32[]{:S(2)}, u32[]{:S(2)}) async-start(f32[8,1,128]{2,1,0:T(1,128)} %bitcast.20), calls=%async_computation.2 | async-start | bytes 8192 | tf_op jit(solution)/shard_map/all_to_all | solution.py:399
  69.0 0.6 bitcast_multiply_fusion
  69.5 0.6 copy.28
  70.2 3.4 %all-to-all-done.2 = f32[8,1,128]{2,1,0:T(1,128)S(1)} async-done(((f32[8,1,128]{2,1,0:T(1,128)}), f32[8,1,128]{2,1,0:T(1,128)S(1)}, u32[]{:S(2)}, u32[]{:S(2)}) %all-to-all-start.2) | async-done | bytes 4128 | tf_op jit(solution)/shard_map/all_to_all | solution.py:399
  73.6 0.6 mixed.1
  (11 shorter events, 0.0 us)
Async XLA Ops:
  0.6 16.5 %copy-start = (f32[16,16,300]{2,1,0:T(8,128)S(1)}, f32[16,16,300]{2,1,0:T(8,128)}, u32[]{:S(2)}) copy-start(f32[16,16,300]{2,1,0:T(8,128)} %param.12) | copy-start | bytes 921604
  0.6 1.0 %copy-start.2 = (bf16[16,2,3072]{2,1,0:T(2,128)(2,1)S(1)}, bf16[16,2,3072]{2,1,0:T(2,128)(2,1)}, u32[]{:S(2)}) copy-start(bf16[16,2,3072]{2,1,0:T(2,128)(2,1)} %green_ref.1) | copy-start | bytes 589828
  1.6 0.7 copy-start.3
  3.8 19.7 %collective-permute-start = (bf16[16,3072]{1,0:T(8,128)(2,1)S(1)}, bf16[16,3072]{1,0:T(8,128)(2,1)S(1)}, u32[]{:S(2)}, u32[]{:S(2)}) collective-permute-start(bf16[16,3072]{1,0:T(8,128)(2,1)S(1)} %get-tuple-element.12), channel_id=1, source_target_pairs={{0,1},{1,2},{2,3},{3,4},{4,5},{5,6},{6,7},{7,8},{8,9},{9,10},{10,1... | collective-permute-start | bytes 294920 | tf_op jit(solution)/shard_map/ppermute | solution.py:382
  6.0 17.5 %collective-permute-start.1 = (bf16[16,3072]{1,0:T(8,128)(2,1)S(1)}, bf16[16,3072]{1,0:T(8,128)(2,1)S(1)}, u32[]{:S(2)}, u32[]{:S(2)}) collective-permute-start(bf16[16,3072]{1,0:T(8,128)(2,1)S(1)} %get-tuple-element.13), channel_id=1, source_target_pairs={{0,31},{1,0},{2,1},{3,2},{4,3},{5,4},{6,5},{7,6},{8,7},{9,8},{10,9... | collective-permute-start | bytes 294920 | tf_op jit(solution)/shard_map/ppermute | solution.py:382
  12.8 10.7 %collective-permute-start.2 = (bf16[16,3072]{1,0:T(8,128)(2,1)S(1)}, bf16[16,3072]{1,0:T(8,128)(2,1)S(1)}, u32[]{:S(2)}, u32[]{:S(2)}) collective-permute-start(bf16[16,3072]{1,0:T(8,128)(2,1)S(1)} %get-tuple-element.14), channel_id=1, source_target_pairs={{0,16},{1,17},{2,18},{3,19},{4,20},{5,21},{6,22},{7,23},{8,24},{9,... | collective-permute-start | bytes 294920 | tf_op jit(solution)/shard_map/ppermute | solution.py:382
  22.6 3.6 %copy-start.1 = (bf16[4,300,3072]{2,1,0:T(8,128)(2,1)}, bf16[4,300,3072]{2,1,0:T(8,128)(2,1)S(1)}, u32[]{:S(2)}) copy-start(bf16[4,300,3072]{2,1,0:T(8,128)(2,1)S(1)} %copy.21.refs_1_.refs_4_) | copy-start | bytes 22118404
  26.2 15.2 %all-to-all-start = ((f32[32,10,1,128]{3,2,1,0:T(1,128)}), f32[32,10,1,128]{3,2,1,0:T(1,128)S(1)}, u32[]{:S(2)}, u32[]{:S(2)}) async-start(f32[32,10,1,128]{3,2,1,0:T(1,128)} %bitcast.2), calls=%async_computation | async-start | bytes 327680 | tf_op jit(solution)/shard_map/all_to_all | solution.py:392
  30.2 21.4 %copy-start.4 = (f32[16]{0:T(128)S(1)}, f32[16]{0:T(128)}, u32[]{:S(2)}) copy-start(f32[16]{0:T(128)} %param.13) | copy-start | bytes 196
  42.6 17.9 %all-to-all-start.1 = ((f32[32,4,1,128]{3,1,2,0:T(4,128)}), f32[32,4,1,128]{3,1,2,0:T(4,128)S(1)}, u32[]{:S(2)}, u32[]{:S(2)}) async-start(f32[32,4,1,128]{3,1,2,0:T(4,128)} %bitcast.6), calls=%async_computation.1 | async-start | bytes 131072 | tf_op jit(solution)/shard_map/all_to_all | solution.py:395
  61.5 12.1 %all-to-all-start.2 = ((f32[8,1,128]{2,1,0:T(1,128)}), f32[8,1,128]{2,1,0:T(1,128)S(1)}, u32[]{:S(2)}, u32[]{:S(2)}) async-start(f32[8,1,128]{2,1,0:T(1,128)} %bitcast.20), calls=%async_computation.2 | async-start | bytes 8192 | tf_op jit(solution)/shard_map/all_to_all | solution.py:399
